TPU v7x, 256 devices: a whole 4x4x8 slice. The times are simulated.
256 devices in a mesh: pipe: 16 (over y, z_hi, core), expert: 16 (over x, z_lo).
Axes of the slice: x: 4, y: 4, z: 8 (z_hi: 2, z_lo: 4; z = z_hi * 4 + z_lo), core: 2. Of those that a mesh axis runs over, the one named last changes fastest.
Arguments:
- forward_layer_input: bfloat16 [32768, 3584], P(('pipe', 'expert')), may hold values from -6 to 6
- front_ids: int32 [32768, 8], P(('pipe', 'expert')), may hold values from 0 to 255, as said below
- front_gate: bfloat16 [32768, 8], P(('pipe', 'expert')), may hold values from 0.19921875 to 1.5
- forward_norm_gain: float32 [16, 3584], P('pipe'), may hold values from 0.5 to 1.5
- front_w_in: bfloat16 [16, 2, 3584, 2048], P('pipe', None, None, 'expert'), may hold values from -0.09375 to 0.09375
- front_w_down: bfloat16 [16, 2048, 3584], P('pipe', 'expert'), may hold values from -0.1875 to 0.1875
- backward_saved_input: bfloat16 [32768, 3584], P(('pipe', 'expert')), may hold values from -6 to 6
- back_grad: bfloat16 [32768, 3584], P(('pipe', 'expert')), may hold values from -6 to 6
- back_ids: int32 [32768, 8], P(('pipe', 'expert')), may hold values from 0 to 255, as said below
- back_gate: bfloat16 [32768, 8], P(('pipe', 'expert')), may hold values from 0.19921875 to 1.5
- backward_norm_gain: float32 [16, 3584], P('pipe'), may hold values from 0.5 to 1.5
- back_w_in: bfloat16 [16, 2, 3584, 2048], P('pipe', None, None, 'expert'), may hold values from -0.09375 to 0.09375
- back_w_down: bfloat16 [16, 2048, 3584], P('pipe', 'expert'), may hold values from -0.1875 to 0.1875
Outputs:
- next_input: bfloat16 [32768, 3584], P(('pipe', 'expert'))
- next_grad: bfloat16 [32768, 3584], P(('pipe', 'expert'))
Inputs may be any that keep to these rules, and one draw needn't show every extreme that they name: `front_ids`: each row names 8 different experts. Experts 0 to 1 are the section's experts computed here. In the 128 rows of one device each of them is named by at most 32 rows, and in every draw some section has one of them named by exactly 32 rows on every device of that section. `back_ids`: as for front_ids.
All inputs are finite; a program needn't handle non-finite values.
Results may differ from a plain program's by a relative error of at most 0.0055.
Values may be sent and summed in bfloat16 or wider, within the bound.
A program may use at most 128 MiB of HBM per device.

v0:
```python
import jax
import jax.numpy as jnp
from jax import lax
from jax.sharding import PartitionSpec as P

EXP_WIN = 2
CAP = 32


EPS = 1e-06


def passed_along(value, axis, by):
    devices = lax.axis_size(axis)
    pairs = [(i, i + by) for i in range(devices) if 0 <= i + by < devices]
    return lax.ppermute(value, axis, pairs)


def slot_tables(expert_ids, route_gate):
    labels = jnp.arange(EXP_WIN, dtype=jnp.int32)
    match = expert_ids[None, :, :] == labels[:, None, None]
    chosen = jnp.any(match, axis=2)
    weights = jnp.sum(
        jnp.where(match, route_gate.astype(jnp.float32)[None], jnp.float32(0.0)), axis=2
    )
    place = jnp.cumsum(chosen.astype(jnp.int32), axis=1) - 1
    slots = jnp.arange(CAP, dtype=jnp.int32)
    table = chosen[:, None, :] & (place[:, None, :] == slots[None, :, None])
    forward_route_table = table.astype(jnp.float32)
    slot_gate = jnp.sum(forward_route_table * weights[:, None, :], axis=2)
    return (forward_route_table, slot_gate.astype(jnp.bfloat16))


def apply_rms_norm(layer_in, gain):
    values = layer_in.astype(jnp.float32)
    scale = lax.rsqrt(jnp.mean(values * values, axis=-1, keepdims=True) + EPS)
    return (values, scale, (values * scale * gain).astype(jnp.bfloat16))


def times_transposed(left, right):
    return lax.dot_general(
        left, right, (((1,), (1,)), ((), ())), preferred_element_type=jnp.float32
    )


def expert_forward(slot_x, slot_g, w_in, w_down):
    shape = slot_x.shape
    flat = slot_x.reshape(-1, shape[-1])
    gate_pre = jnp.dot(flat, w_in[0], preferred_element_type=jnp.float32)
    up_pre = jnp.dot(flat, w_in[1], preferred_element_type=jnp.float32)
    hidden = (jax.nn.silu(gate_pre) * up_pre * slot_g.reshape(-1, 1).astype(jnp.float32)).astype(
        jnp.bfloat16
    )
    part = jnp.dot(hidden, w_down, preferred_element_type=jnp.float32).astype(jnp.bfloat16)
    return part.reshape(shape)


def expert_backward(slot_x, slot_dy, slot_g, w_in, w_down):
    shape = slot_x.shape
    flat = slot_x.reshape(-1, shape[-1])
    gate_pre = jnp.dot(flat, w_in[0], preferred_element_type=jnp.float32)
    up_pre = jnp.dot(flat, w_in[1], preferred_element_type=jnp.float32)
    grad_h = times_transposed(slot_dy.reshape(-1, shape[-1]), w_down) * slot_g.reshape(
        -1, 1
    ).astype(jnp.float32)
    sig = jax.nn.sigmoid(gate_pre)
    grad_gate = (grad_h * up_pre * sig * (1.0 + gate_pre * (1.0 - sig))).astype(jnp.bfloat16)
    grad_up = (grad_h * gate_pre * sig).astype(jnp.bfloat16)
    part = times_transposed(grad_gate, w_in[0]) + times_transposed(grad_up, w_in[1])
    return part.astype(jnp.bfloat16).reshape(shape)


def gather_into_slots(forward_route_table, rows):
    return jnp.einsum(
        "ecr,rd->ecd",
        forward_route_table.astype(jnp.bfloat16),
        rows,
        preferred_element_type=jnp.float32,
    ).astype(jnp.bfloat16)


def unpack_slots(forward_route_table, totals):
    return jnp.einsum("ecr,ecd->rd", forward_route_table, totals, precision=lax.Precision.HIGHEST)


def local(
    forward_layer_input,
    front_ids,
    front_gate,
    forward_norm_gain,
    front_w_in,
    front_w_down,
    backward_saved_input,
    back_grad,
    back_ids,
    back_gate,
    backward_norm_gain,
    back_w_in,
    back_w_down,
):
    peers = lax.axis_size("expert")
    hidden_partition = peers // EXP_WIN
    forward_route_table, gate_f = slot_tables(front_ids, front_gate)
    forward_float_input, forward_inverse_scale, forward_normalized = apply_rms_norm(
        forward_layer_input, forward_norm_gain[0]
    )
    outgoing_forward_rows = jnp.repeat(
        gather_into_slots(forward_route_table, forward_normalized), hidden_partition, axis=0
    )
    send_g = jnp.repeat(gate_f, hidden_partition, axis=0)
    backward_route_table, gate_b = slot_tables(back_ids, back_gate)
    backward_float_input, backward_inverse_scale, backward_normalized = apply_rms_norm(
        backward_saved_input, backward_norm_gain[0]
    )
    outgoing_backward_rows = jnp.repeat(
        gather_into_slots(backward_route_table, backward_normalized), hidden_partition, axis=0
    )
    send_dy = jnp.repeat(
        gather_into_slots(backward_route_table, back_grad), hidden_partition, axis=0
    )
    send_gb = jnp.repeat(gate_b, hidden_partition, axis=0)
    got_x, got_g = (
        lax.all_to_all(outgoing_forward_rows, "expert", split_axis=0, concat_axis=0, tiled=True),
        lax.all_to_all(send_g, "expert", split_axis=0, concat_axis=0, tiled=True),
    )
    got_xb, got_dy, got_gb = (
        lax.all_to_all(outgoing_backward_rows, "expert", split_axis=0, concat_axis=0, tiled=True),
        lax.all_to_all(send_dy, "expert", split_axis=0, concat_axis=0, tiled=True),
        lax.all_to_all(send_gb, "expert", split_axis=0, concat_axis=0, tiled=True),
    )
    part_f = expert_forward(got_x, got_g, front_w_in[0], front_w_down[0])
    part_b = expert_backward(got_xb, got_dy, got_gb, back_w_in[0], back_w_down[0])
    back_f = lax.all_to_all(part_f, "expert", split_axis=0, concat_axis=0, tiled=True)
    total_f = (
        back_f.astype(jnp.float32)
        .reshape((EXP_WIN, hidden_partition) + back_f.shape[1:])
        .sum(axis=1)
    )
    back_b = lax.all_to_all(part_b, "expert", split_axis=0, concat_axis=0, tiled=True)
    total_b = (
        back_b.astype(jnp.float32)
        .reshape((EXP_WIN, hidden_partition) + back_b.shape[1:])
        .sum(axis=1)
    )
    moe_f = unpack_slots(forward_route_table, total_f)
    moe_b = unpack_slots(backward_route_table, total_b)
    out_f = (forward_float_input + moe_f).astype(jnp.bfloat16)
    backward_gain_vector = backward_norm_gain[0]
    dyf = back_grad.astype(jnp.float32)
    grad_x = (
        dyf
        + backward_inverse_scale * backward_gain_vector * moe_b
        - backward_float_input
        * (backward_inverse_scale * backward_inverse_scale * backward_inverse_scale)
        * jnp.mean(backward_float_input * backward_gain_vector * moe_b, axis=-1, keepdims=True)
    )
    next_input, next_grad = passed_along((out_f, grad_x.astype(jnp.bfloat16)), "pipe", 1)
    return (next_input, next_grad)


def solution(mesh):
    return jax.shard_map(
        local,
        mesh=mesh,
        in_specs=(
            P(("pipe", "expert"), None),
            P(("pipe", "expert"), None),
            P(("pipe", "expert"), None),
            P("pipe", None),
            P("pipe", None, None, "expert"),
            P("pipe", "expert", None),
            P(("pipe", "expert"), None),
            P(("pipe", "expert"), None),
            P(("pipe", "expert"), None),
            P(("pipe", "expert"), None),
            P("pipe", None),
            P("pipe", None, None, "expert"),
            P("pipe", "expert", None),
        ),
        out_specs=(P(("pipe", "expert"), None), P(("pipe", "expert"), None)),
        check_vma=False,
    )
```

profile of v0, /device:TPU:16, one launch (start us, length us, event | category | flops | bytes accessed | tf_op | source)
XLA Modules:
  0.0 532.7 jit_solution(6532763999345123715)
XLA Ops:
  0.6 0.8 fusion.74
  1.4 0.3 reduce_window_sum.18
  1.8 0.7 convert_element_type.127
  2.4 0.7 select_reduce_fusion.2
  3.2 0.6 copy.30
  3.9 8.5 %all-to-all-start.4 = ((bf16[16,1,32]{2,1,0:T(2,128)(2,1)}), bf16[16,1,32]{2,1,0:T(2,128)(2,1)S(1)}, u32[]{:S(2)}, u32[]{:S(2)}) async-start(bf16[16,1,32]{2,1,0:T(2,128)(2,1)} %copy.30), calls=%async_computation.4 | async-start | bytes 16384 | tf_op jit(solution)/shard_map/all_to_all | solution.py:129
  12.3 0.7 fusion.75
  13.0 0.3 reduce_window_sum.17
  13.4 0.7 convert_element_type.114
  14.0 0.7 select_reduce_fusion.3
  14.8 0.6 copy.29
  15.5 4.7 all-to-all-done.4
  20.1 3.5 all-to-all-start.1
  23.6 1.4 convolution_convert_fusion.2
  25.1 6.3 %all-to-all-done.1 = bf16[16,1,32]{2,1,0:T(2,128)(2,1)S(1)} async-done(((bf16[16,1,32]{2,1,0:T(2,128)(2,1)}), bf16[16,1,32]{2,1,0:T(2,128)(2,1)S(1)}, u32[]{:S(2)}, u32[]{:S(2)}) %all-to-all-start.1) | async-done | bytes 1056 | tf_op jit(solution)/shard_map/all_to_all | solution.py:124
  31.4 2.2 broadcast_in_dim.54
  33.5 4.6 all-to-all-start.3
  38.2 0.3 fusion.5
  38.5 0.5 convolution_convert_fusion.1
  39.0 80.9 %all-to-all-done.3 = bf16[16,32,3584]{2,1,0:T(8,128)(2,1)} async-done(((bf16[16,32,3584]{2,1,0:T(8,128)(2,1)}), bf16[16,32,3584]{2,1,0:T(8,128)(2,1)}, u32[]{:S(2)}, u32[]{:S(2)}) %all-to-all-start.3) | async-done | bytes 3670048 | tf_op jit(solution)/shard_map/all_to_all | solution.py:128
  119.9 2.2 broadcast_in_dim.57
  122.1 4.6 all-to-all-start.5
  126.8 0.3 fusion.2
  127.1 0.5 convolution_convert_fusion.3
  127.6 83.3 %all-to-all-done.5 = bf16[16,32,3584]{2,1,0:T(8,128)(2,1)} async-done(((bf16[16,32,3584]{2,1,0:T(8,128)(2,1)}), bf16[16,32,3584]{2,1,0:T(8,128)(2,1)}, u32[]{:S(2)}, u32[]{:S(2)}) %all-to-all-start.5) | async-done | bytes 3670048 | tf_op jit(solution)/shard_map/all_to_all | solution.py:127
  210.8 2.3 broadcast_in_dim.28
  213.1 4.5 all-to-all-start
  217.7 3.5 convolution_multiply_fusion.1
  221.3 3.2 fusion.24
  224.4 9.5 %fusion.18 = f32[512,3584]{1,0:T(8,128)} fusion(f32[512,128]{1,0:T(8,128)S(1)} %convolution_multiply_fusion.1, bf16[512,3584]{1,0:T(8,128)(2,1)} %bitcast.17, bf16[1,2,3584,128]{3,2,1,0:T(8,128)(2,1)} %param.24, f32[512,128]{1,0:T(8,128)S(1)} %fusion.24), kind=kOutput, calls=%fused_computation.36 | convolution fusion | flops 940179456 | bytes 13369344 | tf_op jit(solution)/shard_map/dot_general | solution.py:41
  233.9 6.3 %add_convert_fusion = bf16[512,3584]{1,0:T(8,128)(2,1)} fusion(f32[512,3584]{1,0:T(8,128)} %fusion.18, bf16[1,2,3584,128]{3,2,1,0:T(8,128)(2,1)} %param.24, f32[512,128]{1,0:T(8,128)S(1)} %convolution_multiply_fusion.1, f32[512,128]{1,0:T(8,128)S(1)} %fusion.24), kind=kOutput, calls=%fused_computation.2 | convolution fusion | flops 473825280 | bytes 12451840 | tf_op jit(solution)/shard_map/dot_general | solution.py:41
  240.2 61.4 %all-to-all-done = bf16[16,32,3584]{2,1,0:T(8,128)(2,1)} async-done(((bf16[16,32,3584]{2,1,0:T(8,128)(2,1)}), bf16[16,32,3584]{2,1,0:T(8,128)(2,1)}, u32[]{:S(2)}, u32[]{:S(2)}) %all-to-all-start) | async-done | bytes 3670048 | tf_op jit(solution)/shard_map/all_to_all | solution.py:123
  301.6 4.7 all-to-all-start.6
  306.4 3.4 fusion.34
  309.8 8.0 %convolution_convert_fusion = bf16[512,3584]{1,0:T(8,128)(2,1)} fusion(bf16[512,3584]{1,0:T(8,128)(2,1)} %bitcast.2, bf16[1,128,3584]{2,1,0:T(8,128)(2,1)S(1)} %copy-done, bf16[1,2,3584,128]{3,2,1,0:T(8,128)(2,1)} %param.17, f32[512,128]{1,0:T(8,128)S(1)} %fusion.34, f32[512]{0:T(512)S(1)} %reshape.142), kind=kOutput, calls=%fused_computation.3 | convolution fusion | flops 941817856 | bytes 9439232 | tf_op jit(solution)/shard_map/dot_general | solution.py:54
  317.9 72.2 %all-to-all-done.6 = bf16[16,32,3584]{2,1,0:T(8,128)(2,1)} async-done(((bf16[16,32,3584]{2,1,0:T(8,128)(2,1)}), bf16[16,32,3584]{2,1,0:T(8,128)(2,1)}, u32[]{:S(2)}, u32[]{:S(2)}) %all-to-all-start.6) | async-done | bytes 3670048 | tf_op jit(solution)/shard_map/all_to_all | solution.py:139
  390.1 4.5 all-to-all-start.2
  394.6 2.6 convert_reduce_fusion
  397.2 1.2 fusion.12
  398.4 1.8 fusion.10
  400.2 1.9 collective-permute-start.1
  402.1 95.8 %all-to-all-done.2 = bf16[16,32,3584]{2,1,0:T(8,128)(2,1)} async-done(((bf16[16,32,3584]{2,1,0:T(8,128)(2,1)}), bf16[16,32,3584]{2,1,0:T(8,128)(2,1)}, u32[]{:S(2)}, u32[]{:S(2)}) %all-to-all-start.2) | async-done | bytes 3670048 | tf_op jit(solution)/shard_map/all_to_all | solution.py:133
  497.9 2.6 convert_reduce_fusion.1
  500.5 1.0 fusion.1
  501.6 1.9 collective-permute-start
  503.5 27.4 %collective-permute-done = bf16[128,3584]{1,0:T(8,128)(2,1)S(1)} collective-permute-done((bf16[128,3584]{1,0:T(8,128)(2,1)S(1)}, bf16[128,3584]{1,0:T(8,128)(2,1)S(1)}, u32[]{:S(2)}, u32[]{:S(2)}) %collective-permute-start) | collective-permute-done | bytes 917536 | tf_op jit(solution)/shard_map/ppermute | solution.py:16
  530.9 0.9 copy.33
  531.8 0.9 copy.34
  (32 shorter events, 0.6 us)
Async XLA Ops:
  0.6 309.2 %copy-start = (bf16[1,128,3584]{2,1,0:T(8,128)(2,1)S(1)}, bf16[1,128,3584]{2,1,0:T(8,128)(2,1)}, u32[]{:S(2)}) copy-start(bf16[1,128,3584]{2,1,0:T(8,128)(2,1)} %param.18) | copy-start | bytes 2752516
  3.9 16.3 %all-to-all-start.4 = ((bf16[16,1,32]{2,1,0:T(2,128)(2,1)}), bf16[16,1,32]{2,1,0:T(2,128)(2,1)S(1)}, u32[]{:S(2)}, u32[]{:S(2)}) async-start(bf16[16,1,32]{2,1,0:T(2,128)(2,1)} %copy.30), calls=%async_computation.4 | async-start | bytes 16384 | tf_op jit(solution)/shard_map/all_to_all | solution.py:129
  20.1 11.2 %all-to-all-start.1 = ((bf16[16,1,32]{2,1,0:T(2,128)(2,1)}), bf16[16,1,32]{2,1,0:T(2,128)(2,1)S(1)}, u32[]{:S(2)}, u32[]{:S(2)}) async-start(bf16[16,1,32]{2,1,0:T(2,128)(2,1)} %copy.29), calls=%async_computation.1 | async-start | bytes 16384 | tf_op jit(solution)/shard_map/all_to_all | solution.py:124
  33.5 4.6 copy-start.5
  33.5 4.7 copy-start.1
  33.5 86.3 %all-to-all-start.3 = ((bf16[16,32,3584]{2,1,0:T(8,128)(2,1)}), bf16[16,32,3584]{2,1,0:T(8,128)(2,1)}, u32[]{:S(2)}, u32[]{:S(2)}) async-start(bf16[16,32,3584]{2,1,0:T(8,128)(2,1)} %bitcast.70), calls=%async_computation.3 | async-start | bytes 7340032 | tf_op jit(solution)/shard_map/all_to_all | solution.py:128
  122.1 4.7 copy-start.6
  122.1 4.7 copy-start.3
  122.1 88.8 %all-to-all-start.5 = ((bf16[16,32,3584]{2,1,0:T(8,128)(2,1)}), bf16[16,32,3584]{2,1,0:T(8,128)(2,1)}, u32[]{:S(2)}, u32[]{:S(2)}) async-start(bf16[16,32,3584]{2,1,0:T(8,128)(2,1)} %bitcast.69), calls=%async_computation.5 | async-start | bytes 7340032 | tf_op jit(solution)/shard_map/all_to_all | solution.py:127
  213.1 88.5 %all-to-all-start = ((bf16[16,32,3584]{2,1,0:T(8,128)(2,1)}), bf16[16,32,3584]{2,1,0:T(8,128)(2,1)}, u32[]{:S(2)}, u32[]{:S(2)}) async-start(bf16[16,32,3584]{2,1,0:T(8,128)(2,1)} %bitcast.68), calls=%async_computation | async-start | bytes 7340032 | tf_op jit(solution)/shard_map/all_to_all | solution.py:123
  217.7 3.5 copy-start.2
  301.6 88.5 %all-to-all-start.6 = ((bf16[16,32,3584]{2,1,0:T(8,128)(2,1)}), bf16[16,32,3584]{2,1,0:T(8,128)(2,1)}, u32[]{:S(2)}, u32[]{:S(2)}) async-start(bf16[16,32,3584]{2,1,0:T(8,128)(2,1)} %bitcast.67), calls=%async_computation.6 | async-start | bytes 7340032 | tf_op jit(solution)/shard_map/all_to_all | solution.py:139
  390.1 107.9 %all-to-all-start.2 = ((bf16[16,32,3584]{2,1,0:T(8,128)(2,1)}), bf16[16,32,3584]{2,1,0:T(8,128)(2,1)}, u32[]{:S(2)}, u32[]{:S(2)}) async-start(bf16[16,32,3584]{2,1,0:T(8,128)(2,1)} %bitcast.66), calls=%async_computation.2 | async-start | bytes 7340032 | tf_op jit(solution)/shard_map/all_to_all | solution.py:133
  397.2 1.2 copy-start.4
  400.2 103.3 %collective-permute-start.1 = (bf16[128,3584]{1,0:T(8,128)(2,1)}, bf16[128,3584]{1,0:T(8,128)(2,1)S(1)}, u32[]{:S(2)}, u32[]{:S(2)}) collective-permute-start(bf16[128,3584]{1,0:T(8,128)(2,1)} %fusion.10), channel_id=1, source_target_pairs={{0,16},{16,32},{32,48},{48,64},{64,80},{80,96},{96,112},{112,128},... | collective-permute-start | bytes 2752520 | tf_op jit(solution)/shard_map/ppermute | solution.py:16
  501.6 29.4 %collective-permute-start = (bf16[128,3584]{1,0:T(8,128)(2,1)S(1)}, bf16[128,3584]{1,0:T(8,128)(2,1)S(1)}, u32[]{:S(2)}, u32[]{:S(2)}) collective-permute-start(bf16[128,3584]{1,0:T(8,128)(2,1)S(1)} %fusion.1), channel_id=1, source_target_pairs={{0,16},{16,32},{32,48},{48,64},{64,80},{80,96},{96,112},{112,128},... | collective-permute-start | bytes 2752520 | tf_op jit(solution)/shard_map/ppermute | solution.py:16
where the time goes:
time: 534 us; the launch traced here: 533 us
  waiting for transfers between devices  432 us (81%)
  starting transfers between devices  38.7 us (7%)
  matrix products  38.5 us (7%)
  other arithmetic  12.8 us (2%)
  local copies, waits for them, and re-layouts  9.92 us (2%)
    all_to_all x1, waiting for transfers between devices, local(): lax.all_to_all(part_f, 'expert', split_axis=0, concat_axis=0, tiled=True)  95.8 us
    all_to_all x1, waiting for transfers between devices, local(): lax.all_to_all(outgoing_backward_rows, 'expert', split_axis=0, concat_axi...  83.3 us
    all_to_all x1, waiting for transfers between devices, local(): lax.all_to_all(send_dy, 'expert', split_axis=0, concat_axis=0, tiled=True)  80.9 us
    all_to_all x1, waiting for transfers between devices, local(): lax.all_to_all(part_b, 'expert', split_axis=0, concat_axis=0, tiled=True)  72.2 us
    all_to_all x1, waiting for transfers between devices, local(): lax.all_to_all(outgoing_forward_rows, 'expert', split_axis=0, concat_axis...  61.4 us
    ppermute x2, waiting for transfers between devices, passed_along(): return lax.ppermute(value, axis, pairs)  27.4 us
    dot_general x3, matrix products, times_transposed(): lax.dot_general(left, right, (((1,), (1,)), ((), ())), preferred_element_...  19.3 us
  transfers between devices with their start and end apart: 9, of which 8 were waited for; matrix products, arithmetic and copies ran while one was open for 9% of the time, Pallas kernels for 0%

commit v1 on v0

v1 whole, which is shorter than its diff:
```python
import functools

import jax
import jax.numpy as jnp
from jax import lax
from jax.experimental import pallas as pl
from jax.experimental.pallas import tpu as pltpu
from jax.sharding import PartitionSpec as P

MESH = pl.DeviceIdType.MESH
F32 = jnp.float32
BF16 = jnp.bfloat16

D = 3584
CAP = 32
TOK = 128
HID = 128
NZ = 4
NC = 7
CW = D // NC
KC = 896
EPS = 1e-06


def dot(a, b):
    return jnp.dot(a, b, preferred_element_type=F32)


def dot_t(a, b):
    return lax.dot_general(a, b, (((1,), (1,)), ((), ())), preferred_element_type=F32)


def kernel(
    x_ref, idf_ref, gf_ref, gainf_ref, winf_ref, wdf_ref,
    xb_ref, dy_ref, idb_ref, gb_ref, gainb_ref, winb_ref, wdb_ref,
    outf_ref, outb_ref,
    xf_v, xb_v, dy_v, xh, rinv, tg_f, tg_b,
    wgu_b, wd_b, wgu_f, wd_f,
    g_b, g_f, x_b, x_f, p_b, p_f, r_b, r_f, tot_b, tot_f,
    acc, accd, hid, moe, o_b, o_f, zero,
    lsem, ws, wr, gs_b, gr_b, gs_f, gr_f, xs, rs_b, rr_b, rs_f, rr_f,
    ts_b, tr_b, ts_f, tr_f, os_b, or_b, os_f, or_f, zsem,
):
    p = lax.axis_index("pipe")
    e = lax.axis_index("expert")
    n_pipe = lax.axis_size("pipe")
    xq = e // NZ
    z = lax.rem(e, NZ)
    mine = xq // 2
    pair = (p, e + NZ - 2 * NZ * lax.rem(xq, 2))
    cross = (p, (3 - xq) * NZ + z)
    right = (p, e + 1)
    left = (p, e - 1)
    ahead = (p + 1, e)
    behind = (p - 1, e)
    has_l, has_r = z > 0, z < NZ - 1
    has_prev, has_next = p > 0, p < n_pipe - 1

    def remote(src, dst, ssem, rsem, dev):
        return pltpu.make_async_remote_copy(
            src_ref=src, dst_ref=dst, send_sem=ssem, recv_sem=rsem,
            device_id=dev, device_id_type=MESH,
        )

    loads = [
        pltpu.make_async_copy(xb_ref, xb_v, lsem.at[0]),
        pltpu.make_async_copy(dy_ref, dy_v, lsem.at[1]),
        pltpu.make_async_copy(x_ref, xf_v, lsem.at[2]),
        pltpu.make_async_copy(winb_ref.at[0, 0], wgu_b.at[0, :, pl.ds(0, HID)], lsem.at[3]),
        pltpu.make_async_copy(winb_ref.at[0, 1], wgu_b.at[0, :, pl.ds(HID, HID)], lsem.at[4]),
        pltpu.make_async_copy(wdb_ref.at[0], wd_b.at[pl.ds(0, HID)], lsem.at[5]),
        pltpu.make_async_copy(winf_ref.at[0, 0], wgu_f.at[0, :, pl.ds(0, HID)], lsem.at[6]),
        pltpu.make_async_copy(winf_ref.at[0, 1], wgu_f.at[0, :, pl.ds(HID, HID)], lsem.at[7]),
        pltpu.make_async_copy(wdf_ref.at[0], wd_f.at[pl.ds(0, HID)], lsem.at[8]),
    ]
    for c in loads:
        c.start()

    bar = pltpu.get_barrier_semaphore()

    def greet(dev):
        pl.semaphore_signal(bar, inc=1, device_id=dev, device_id_type=MESH)

    greet(pair)
    greet(cross)
    pl.when(has_l)(lambda: greet(left))
    pl.when(has_r)(lambda: greet(right))
    pl.when(has_prev)(lambda: greet(behind))
    pl.when(has_next)(lambda: greet(ahead))
    count = (
        2 + has_l.astype(jnp.int32) + has_r.astype(jnp.int32)
        + has_prev.astype(jnp.int32) + has_next.astype(jnp.int32)
    )
    pl.semaphore_wait(bar, count)

    weights = [
        remote(winb_ref.at[0, 0], wgu_b.at[1, :, pl.ds(0, HID)], ws.at[0], wr.at[0], pair),
        remote(winb_ref.at[0, 1], wgu_b.at[1, :, pl.ds(HID, HID)], ws.at[1], wr.at[1], pair),
        remote(wdb_ref.at[0], wd_b.at[pl.ds(HID, HID)], ws.at[2], wr.at[2], pair),
        remote(winf_ref.at[0, 0], wgu_f.at[1, :, pl.ds(0, HID)], ws.at[3], wr.at[3], pair),
        remote(winf_ref.at[0, 1], wgu_f.at[1, :, pl.ds(HID, HID)], ws.at[4], wr.at[4], pair),
        remote(wdf_ref.at[0], wd_f.at[pl.ds(HID, HID)], ws.at[5], wr.at[5], pair),
    ]
    for c in weights:
        c.start()

    def table(ids_ref, gate_ref, tg):
        ids = ids_ref[...]
        gate = gate_ref[...].astype(F32)
        lane = lax.broadcasted_iota(jnp.int32, (TOK, TOK), 1)
        row = lax.broadcasted_iota(jnp.int32, (TOK, TOK), 0)
        hits = jnp.zeros((TOK, TOK), F32)
        weight = jnp.zeros((TOK, TOK), F32)
        for i, expert in enumerate((mine, 1 - mine)):
            match = ids == expert
            hit = jnp.max(jnp.where(match, 1.0, 0.0), axis=1, keepdims=True)
            w = jnp.sum(jnp.where(match, gate, 0.0), axis=1, keepdims=True)
            here = (lane >= CAP * i) & (lane < CAP * (i + 1))
            hits = jnp.where(here, hit, hits)
            weight = jnp.where(here, w, weight)
        lower = jnp.where(row >= lane, 1.0, 0.0).astype(BF16)
        order = dot(lower, hits.astype(BF16))
        slot = ((lane & (CAP - 1)) + 1).astype(F32)
        tab = jnp.where(order == slot, hits, 0.0)
        tg[...] = (tab * weight).astype(BF16)[:, : 2 * CAP]
        return tab.T.astype(BF16)[: 2 * CAP]

    def normalise(src, gain_ref, keep):
        @pl.loop(0, TOK // 16)
        def _(i):
            rows = pl.ds(pl.multiple_of(i * 16, 16), 16)
            v = src[rows, :].astype(F32)
            r = lax.rsqrt(jnp.sum(v * v, axis=1, keepdims=True) * (1.0 / D) + EPS)
            xh[rows, :] = (v * r * gain_ref[...]).astype(BF16)
            if keep:
                rinv[rows, :] = jnp.broadcast_to(r, (16, TOK))

    def cols_of(c, width):
        return pl.ds(pl.multiple_of(c * width, width), width)

    def pick(tab, src, own_at, cross_at):
        @pl.loop(0, NC)
        def _(c):
            cols = cols_of(c, CW)
            s = dot(tab, src[:, cols]).astype(BF16)
            own_at(cols, s[:CAP])
            cross_at(cols, s[CAP:])

    def own_b(a):
        def put(cols, v):
            g_b[a, 2 * z, :, cols] = v
        return put

    def cross_b(a):
        def put(cols, v):
            x_b[a, :, cols] = v
        return put

    def own_f(cols, v):
        g_f[2 * z, :, cols] = v

    def cross_f(cols, v):
        x_f[:, cols] = v

    def gb_copy(b, way):
        return remote(
            g_b.at[:, b], g_b.at[:, b], gs_b.at[way, b], gr_b.at[b], (left, right)[way]
        )

    def gf_copy(b, way):
        return remote(g_f.at[b], g_f.at[b], gs_f.at[way, b], gr_f.at[b], (left, right)[way])

    def both_ways(copy, b):
        pl.when(has_r)(lambda: copy(b, 1).start())
        pl.when(has_l)(lambda: copy(b, 0).start())

    def gather_step(copy, k):
        for s in range(2):
            @pl.when(z >= k)
            def _():
                b = 2 * (z - k) + s
                copy(b, 1).wait_recv()
                pl.when(has_r)(lambda: copy(b, 1).start())

            @pl.when(z + k < NZ)
            def _():
                b = 2 * (z + k) + s
                copy(b, 0).wait_recv()
                pl.when(has_l)(lambda: copy(b, 0).start())

    def gather_drain(copy):
        for k in range(NZ):
            for s in range(2):
                @pl.when((z >= k) & has_r)
                def _():
                    copy(2 * (z - k) + s, 1).wait_send()

                @pl.when((z + k < NZ) & has_l)
                def _():
                    copy(2 * (z + k) + s, 0).wait_send()

    xb_copy = remote(x_b, g_b.at[:, 2 * z + 1], xs.at[0], gr_b.at[2 * z + 1], cross)
    xf_copy = remote(x_f, g_f.at[2 * z + 1], xs.at[1], gr_f.at[2 * z + 1], cross)

    tab = table(idb_ref, gb_ref, tg_b)
    loads[1].wait()
    pick(tab, dy_v, own_b(1), cross_b(1))
    loads[0].wait()
    normalise(xb_v, gainb_ref, True)
    pick(tab, xh, own_b(0), cross_b(0))
    xb_copy.start()
    both_ways(gb_copy, 2 * z)

    tab = table(idf_ref, gf_ref, tg_f)
    loads[2].wait()
    normalise(xf_v, gainf_ref, False)
    pick(tab, xh, own_f, cross_f)
    xf_copy.start()

    @pl.when(jnp.logical_not(has_prev))
    def _():
        @pl.loop(0, TOK // 16)
        def _(i):
            zero[pl.ds(pl.multiple_of(i * 16, 16), 16), :] = jnp.zeros((16, D), BF16)
        for i, out in enumerate((outf_ref, outb_ref)):
            pltpu.make_async_copy(zero, out, zsem.at[i]).start()

    xb_copy.wait_recv()
    both_ways(gb_copy, 2 * z + 1)
    gather_step(gb_copy, 1)
    gather_step(gb_copy, 2)
    both_ways(gf_copy, 2 * z)
    xf_copy.wait_recv()
    both_ways(gf_copy, 2 * z + 1)
    gather_step(gb_copy, 3)

    def reducer(part, got, ssem, rsem, chunked):
        def at(d, c):
            return (d, slice(None), cols_of(c, CW)) if chunked else (d,)

        def copy(d, way, c):
            i = (d, c) if chunked else (d,)
            return remote(
                part.at[at(d, c)], got.at[(1 - way,) + at(d, c)],
                ssem.at[i], rsem.at[(1 - way,) + i], (left, right)[way],
            )

        def add(d, side, c):
            if chunked:
                cols = cols_of(c, CW)
                part[d, :, cols] = (
                    part[d, :, cols].astype(F32) + got[side, d, :, cols].astype(F32)
                ).astype(BF16)
            else:
                pl.loop(0, NC)(lambda i: add_cols(d, side, cols_of(i, CW)))

        def add_cols(d, side, cols):
            part[d, :, cols] = (
                part[d, :, cols].astype(F32) + got[side, d, :, cols].astype(F32)
            ).astype(BF16)

        def edge(c):
            @pl.when(z == 0)
            def _():
                for d in range(NZ - 1, 0, -1):
                    copy(d, 1, c).start()

            @pl.when(z == NZ - 1)
            def _():
                for d in range(NZ - 1):
                    copy(d, 0, c).start()

        def relay(c, k):
            d = NZ - 1 - k

            @pl.when((z > 0) & (z < d))
            def _():
                copy(d, 1, c).wait_recv()
                add(d, 0, c)
                copy(d, 1, c).start()

            @pl.when((z < NZ - 1) & (z > k))
            def _():
                copy(k, 0, c).wait_recv()
                add(k, 1, c)
                copy(k, 0, c).start()

        def own(c):
            @pl.when(has_l)
            def _():
                copy(z, 1, c).wait_recv()
                add(z, 0, c)

            @pl.when(has_r)
            def _():
                copy(z, 0, c).wait_recv()
                add(z, 1, c)

        def drain(c):
            for d in range(NZ):
                pl.when(z < d)(lambda: copy(d, 1, c).wait_send())
                pl.when(z > d)(lambda: copy(d, 0, c).wait_send())

        return edge, relay, own, drain

    edge_b, relay_b, sum_b, drain_b = reducer(p_b, r_b, rs_b, rr_b, False)
    edge_f, relay_f, sum_f, drain_f = reducer(p_f, r_f, rs_f, rr_f, True)

    def totals_b():
        return remote(
            p_b.at[z, pl.ds(CAP, CAP)], tot_b, ts_b.at[0], tr_b.at[0], cross
        )

    def totals_f(c):
        cols = cols_of(c, CW)
        return remote(
            p_f.at[z, pl.ds(CAP, CAP), cols], tot_f.at[:, cols], ts_f.at[c], tr_f.at[c], cross
        )

    def shift_b():
        return remote(o_b, outb_ref, os_b.at[0], or_b.at[0], ahead)

    def shift_f(c):
        cols = cols_of(c, CW)
        return remote(o_f.at[:, cols], outf_ref.at[:, cols], os_f.at[c], or_f.at[c], ahead)

    for i in (3, 4, 5):
        loads[i].wait()
    for i in (0, 1, 2):
        weights[i].wait_recv()
    acc[...] = jnp.zeros_like(acc)
    accd[...] = jnp.zeros_like(accd)

    @pl.loop(0, D // KC)
    def _(c):
        cols = cols_of(c, KC)
        xs_c = g_b[0, :, :, cols].reshape(2 * NZ * CAP, KC)
        dy_c = g_b[1, :, :, cols].reshape(2 * NZ * CAP, KC)
        for o in range(2):
            acc[o] += dot(xs_c, wgu_b[o, cols, :])
        accd[...] += dot_t(dy_c, wd_b[:, cols])

    for o in range(2):
        a = acc[o, :, :HID]
        b = acc[o, :, HID:]
        dh = accd[:, o * HID : (o + 1) * HID]
        sg = jax.nn.sigmoid(a)
        hid[o, :, :HID] = (dh * b * sg * (1.0 + a * (1.0 - sg))).astype(BF16)
        hid[o, :, HID:] = (dh * a * sg).astype(BF16)

    @pl.loop(0, NC)
    def _(c):
        cols = cols_of(c, CW)
        part = dot_t(hid[0], wgu_b[0, cols, :]) + dot_t(hid[1], wgu_b[1, cols, :])
        p_b[:, :, cols] = part.astype(BF16).reshape(NZ, 2 * CAP, CW)

    edge_b(0)
    gather_step(gf_copy, 1)
    relay_b(0, 0)
    gather_step(gf_copy, 2)
    relay_b(0, 1)
    relay_b(0, 2)
    gather_step(gf_copy, 3)
    sum_b(0)
    totals_b().start()

    for i in (6, 7, 8):
        loads[i].wait()
    for i in (3, 4):
        weights[i].wait_recv()
    acc[...] = jnp.zeros_like(acc)

    @pl.loop(0, D // KC)
    def _(c):
        cols = cols_of(c, KC)
        xs_c = g_f[:, :, cols].reshape(2 * NZ * CAP, KC)
        for o in range(2):
            acc[o] += dot(xs_c, wgu_f[o, cols, :])

    for o in range(2):
        a = acc[o, :, :HID]
        hid[0, :, o * HID : (o + 1) * HID] = (
            a * jax.nn.sigmoid(a) * acc[o, :, HID:]
        ).astype(BF16)

    def finish_b():
        totals_b().wait_recv()

        def moe_cols(c, total):
            cols = cols_of(c, CW)
            rows = jnp.concatenate([p_b[z, pl.ds(0, CAP), cols], tot_b[:, cols]], axis=0)
            m = dot(tg_b[...], rows) * gainb_ref[:, cols]
            moe[:, cols] = m
            return total + jnp.sum(xb_v[:, cols].astype(F32) * m, axis=1, keepdims=True)

        total = lax.fori_loop(0, NC, moe_cols, jnp.zeros((TOK, 1), F32))
        r = rinv[:, :1]
        scale = r * r * r * (total * (1.0 / D))

        @pl.loop(0, NC)
        def _(c):
            cols = cols_of(c, CW)
            o_b[:, cols] = (
                dy_v[:, cols].astype(F32) + r * moe[:, cols] - xb_v[:, cols].astype(F32) * scale
            ).astype(BF16)

        pl.when(has_next)(lambda: shift_b().start())

    def part_f(c):
        cols = cols_of(c, CW)
        p_f[:, :, cols] = dot(hid[0], wd_f[:, cols]).astype(BF16).reshape(NZ, 2 * CAP, CW)

    def finish_f(c):
        totals_f(c).wait_recv()
        cols = cols_of(c, CW)
        rows = jnp.concatenate([p_f[z, pl.ds(0, CAP), cols], tot_f[:, cols]], axis=0)
        o_f[:, cols] = (xf_v[:, cols].astype(F32) + dot(tg_f[...], rows)).astype(BF16)
        pl.when(has_next)(lambda: shift_f(c).start())

    weights[5].wait_recv()

    @pl.loop(0, NC + 3)
    def _(i):
        @pl.when(i < NC)
        def _():
            part_f(i)
            edge_f(i)

        pl.when(i == 1)(finish_b)

        @pl.when((i >= 1) & (i < NC + 1))
        def _():
            for k in range(NZ - 1):
                relay_f(i - 1, k)

        @pl.when((i >= 2) & (i < NC + 2))
        def _():
            sum_f(i - 2)
            totals_f(i - 2).start()

        pl.when(i >= 3)(lambda: finish_f(i - 3))

    for c in weights:
        c.wait_send()
    xb_copy.wait_send()
    xf_copy.wait_send()
    gather_drain(gb_copy)
    gather_drain(gf_copy)
    drain_b(0)
    totals_b().wait_send()

    @pl.loop(0, NC)
    def _(c):
        drain_f(c)
        totals_f(c).wait_send()
        pl.when(has_next)(lambda: shift_f(c).wait_send())
        pl.when(has_prev)(lambda: shift_f(c).wait_recv())

    pl.when(has_next)(lambda: shift_b().wait_send())
    pl.when(has_prev)(lambda: shift_b().wait_recv())

    @pl.when(jnp.logical_not(has_prev))
    def _():
        for i, out in enumerate((outf_ref, outb_ref)):
            pltpu.make_async_copy(zero, out, zsem.at[i]).wait()


def local(*args):
    hbm = pl.BlockSpec(memory_space=pl.ANY)
    vmem = pl.BlockSpec(memory_space=pltpu.VMEM)
    dma = pltpu.SemaphoreType.DMA
    blocks = 2 * NZ
    rows = blocks * CAP
    return pl.pallas_call(
        kernel,
        out_shape=[jax.ShapeDtypeStruct((TOK, D), BF16)] * 2,
        in_specs=[
            hbm, vmem, vmem, vmem, hbm, hbm,
            hbm, hbm, vmem, vmem, vmem, hbm, hbm,
        ],
        out_specs=[hbm, hbm],
        scratch_shapes=[
            pltpu.VMEM((TOK, D), BF16),
            pltpu.VMEM((TOK, D), BF16),
            pltpu.VMEM((TOK, D), BF16),
            pltpu.VMEM((TOK, D), BF16),
            pltpu.VMEM((TOK, TOK), F32),
            pltpu.VMEM((TOK, 2 * CAP), BF16),
            pltpu.VMEM((TOK, 2 * CAP), BF16),
            pltpu.VMEM((2, D, 2 * HID), BF16),
            pltpu.VMEM((2 * HID, D), BF16),
            pltpu.VMEM((2, D, 2 * HID), BF16),
            pltpu.VMEM((2 * HID, D), BF16),
            pltpu.VMEM((2, blocks, CAP, D), BF16),
            pltpu.VMEM((blocks, CAP, D), BF16),
            pltpu.VMEM((2, CAP, D), BF16),
            pltpu.VMEM((CAP, D), BF16),
            pltpu.VMEM((NZ, 2 * CAP, D), BF16),
            pltpu.VMEM((NZ, 2 * CAP, D), BF16),
            pltpu.VMEM((2, NZ, 2 * CAP, D), BF16),
            pltpu.VMEM((2, NZ, 2 * CAP, D), BF16),
            pltpu.VMEM((CAP, D), BF16),
            pltpu.VMEM((CAP, D), BF16),
            pltpu.VMEM((2, rows, 2 * HID), F32),
            pltpu.VMEM((rows, 2 * HID), F32),
            pltpu.VMEM((2, rows, 2 * HID), BF16),
            pltpu.VMEM((TOK, D), F32),
            pltpu.VMEM((TOK, D), BF16),
            pltpu.VMEM((TOK, D), BF16),
            pltpu.VMEM((TOK, D), BF16),
            dma((9,)),
            dma((6,)),
            dma((6,)),
            dma((2, blocks)),
            dma((blocks,)),
            dma((2, blocks)),
            dma((blocks,)),
            dma((2,)),
            dma((NZ,)),
            dma((2, NZ)),
            dma((NZ, NC)),
            dma((2, NZ, NC)),
            dma((1,)),
            dma((1,)),
            dma((NC,)),
            dma((NC,)),
            dma((1,)),
            dma((1,)),
            dma((NC,)),
            dma((NC,)),
            dma((2,)),
        ],
        compiler_params=pltpu.CompilerParams(
            collective_id=0, has_side_effects=True, vmem_limit_bytes=56 * 2**20
        ),
        cost_estimate=pl.CostEstimate(
            flops=4 * 10**9, bytes_accessed=16 * 10**6, transcendentals=10**5
        ),
    )(*args)


def solution(mesh):
    tokens = P(("pipe", "expert"), None)
    w_in = P("pipe", None, None, "expert")
    w_down = P("pipe", "expert", None)
    gain = P("pipe", None)
    return jax.shard_map(
        local,
        mesh=mesh,
        in_specs=(
            tokens, tokens, tokens, gain, w_in, w_down,
            tokens, tokens, tokens, tokens, gain, w_in, w_down,
        ),
        out_specs=(tokens, tokens),
        check_vma=False,
    )
```

time: 534 us -> 237 us (0.44)
  waiting for transfers between devices: 432 us -> 0 us
  Pallas kernels: 0 us -> 223 us
  starting transfers between devices: 38.7 us -> 0 us
  matrix products: 38.5 us -> 0 us
  other arithmetic: 12.8 us -> 0 us
    all_to_all x7 -> x0, waiting for transfers between devices: 405 us -> none  [the longest x1 95.8 us: local(): lax.all_to_all(part_f, 'expert', split_axis=0, concat_axis=0, tiled=True)]
    pallas_call x0 -> x1, Pallas kernels: none -> 223 us  [local(): pl.pallas_call(kernel, out_shape=[jax.ShapeDtypeStruct((TOK, D), BF16)] *...]
    dot_general x11 -> x0, matrix products: 38.5 us -> none  [the longest x3 19.3 us: times_transposed(): lax.dot_general(left, right, (((1,), (1,)), ((), ())), preferred_element_...]
    all_to_all x7 -> x0, starting transfers between devices: 34.9 us -> none  [the longest x1 8.47 us: local(): lax.all_to_all(send_gb, 'expert', split_axis=0, concat_axis=0, tiled=True)]
    ppermute x2 -> x0, waiting for transfers between devices: 27.4 us -> none  [passed_along(): return lax.ppermute(value, axis, pairs)]
    reduce_sum x8 -> x0, other arithmetic: 7.39 us -> none  [the longest x1 2.63 us: local(): total_b = back_b.astype(jnp.float32).reshape((EXP_WIN, hidden_partition)...]
    unnamed x16 -> x8, local copies, waits for them, and re-layouts: 1.88 us -> 8.76 us
    broadcast_in_dim x3 -> x0, local copies, waits for them, and re-layouts: 6.65 us -> none  [the longest x1 2.27 us: local(): jnp.repeat(gather_into_slots(forward_route_table, forward_normalized), hi...]
  transfers between devices with their start and end apart: 9 -> 0, of which waited for: 8 -> 0; matrix products, arithmetic and copies ran while one was open for 9% -> 0% of each run, Pallas kernels for 0% -> 0%
where the time goes in v1:
time: 237 us; the launch traced here: 232 us
  Pallas kernels  223 us (94%)
  local copies, waits for them, and re-layouts  8.76 us (4%)
    pallas_call x1, Pallas kernels, local(): pl.pallas_call(kernel, out_shape=[jax.ShapeDtypeStruct((TOK, D), BF16)] *...  223 us
    unnamed x8, local copies, waits for them, and re-layouts  8.76 us

profile of v1, /device:TPU:16, one launch (start us, length us, event | category | flops | bytes accessed | tf_op | source)
XLA Modules:
  0.0 232.3 jit_solution(11563603933286463215)
XLA Ops:
  0.6 1.4 copy.16.gf_ref
  2.0 1.4 copy.18.gb_ref
  3.4 1.4 copy.15.idf_ref
  4.8 1.4 copy.17.idb_ref
  6.2 222.9 %shard_map.140 = (bf16[128,3584]{1,0:T(8,128)(2,1)}, bf16[128,3584]{1,0:T(8,128)(2,1)}) custom-call(bf16[128,3584]{1,0:T(8,128)(2,1)} %x_ref.1, s32[128,8]{1,0:T(8,128)} %copy.15.idf_ref, bf16[128,8]{1,0:T(8,128)(2,1)} %copy.16.gf_ref, f32[1,3584]{1,0:T(1,128)} %gainf_ref.1, bf16[1,2,3584,128]{3,2,1,0:T(8,128)(2,1)} %winf_ref.1, ...), custom_call_target="tpu_custom_call" | custom-call | flops 4000000000 | bytes 16000000 | tf_op jit(solution)/shard_map/pallas_call | solution.py:474
  229.1 0.0 copy-start
  229.1 2.2 copy.21
  231.3 0.0 copy-done
  231.3 0.9 copy.22
Async XLA Ops:
  229.1 2.3 copy-start

commit v2 on v1

v2 whole, which is shorter than its diff:
```python
import functools

import jax
import jax.numpy as jnp
from jax import lax
from jax.experimental import pallas as pl
from jax.experimental.pallas import tpu as pltpu
from jax.sharding import PartitionSpec as P

MESH = pl.DeviceIdType.MESH
F32 = jnp.float32
BF16 = jnp.bfloat16

D = 3584
CAP = 32
TOK = 128
HID = 128
NZ = 4
NC = 4
CW = D // NC
KC = 896
EPS = 1e-06
GAP = 0
ST = 1
FB = 0
TURN_AT = 2
W0_AT = 1
F_AT = (0, 1, 3)


def dot(a, b):
    return jnp.dot(a, b, preferred_element_type=F32)


def dot_t(a, b):
    return lax.dot_general(a, b, (((1,), (1,)), ((), ())), preferred_element_type=F32)


def kernel(
    x_ref, idf_ref, gf_ref, gainf_ref, winf_ref, wdf_ref,
    xb_ref, dy_ref, idb_ref, gb_ref, gainb_ref, winb_ref, wdb_ref,
    outf_ref, outb_ref,
    xf_v, xb_v, dy_v, xh, rinv, tg_f, tg_b,
    wgu_b, wd_b, wgu_f, wd_f,
    blk, crs, part, got, tot,
    acc, accd, hid, moe, o_b, o_f, zero,
    lsem, ws, wr, gs, gr, xs, rs, rr, ts, tr, os_b, or_b, os_f, or_f, zsem, turn,
):
    p = lax.axis_index("pipe")
    e = lax.axis_index("expert")
    n_pipe = lax.axis_size("pipe")
    xq = e // NZ
    z = lax.rem(e, NZ)
    mine = xq // 2
    pair = (p, e + NZ - 2 * NZ * lax.rem(xq, 2))
    cross = (p, (3 - xq) * NZ + z)
    right = (p, e + 1)
    left = (p, e - 1)
    ahead = (p + 1, e)
    behind = (p - 1, e)
    has_l, has_r = z > 0, z < NZ - 1
    has_prev, has_next = p > 0, p < n_pipe - 1
    first = lax.rem(p, 2) == 1

    def remote(src, dst, ssem, rsem, dev):
        return pltpu.make_async_remote_copy(
            src_ref=src, dst_ref=dst, send_sem=ssem, recv_sem=rsem,
            device_id=dev, device_id_type=MESH,
        )

    bar = pltpu.get_barrier_semaphore()

    def greet(dev):
        pl.semaphore_signal(bar, inc=1, device_id=dev, device_id_type=MESH)

    greet(pair)
    greet(cross)
    pl.when(has_l)(lambda: greet(left))
    pl.when(has_r)(lambda: greet(right))
    pl.when(has_prev)(lambda: greet(behind))
    pl.when(has_next)(lambda: greet(ahead))

    loads = [
        pltpu.make_async_copy(dy_ref, dy_v, lsem.at[0]),
        pltpu.make_async_copy(xb_ref, xb_v, lsem.at[1]),
        pltpu.make_async_copy(x_ref, xf_v, lsem.at[2]),
        pltpu.make_async_copy(winb_ref.at[0], wgu_b.at[0], lsem.at[3]),
        pltpu.make_async_copy(wdb_ref.at[0], wd_b.at[pl.ds(0, HID)], lsem.at[4]),
        pltpu.make_async_copy(winf_ref.at[0], wgu_f.at[0], lsem.at[5]),
        pltpu.make_async_copy(wdf_ref.at[0], wd_f.at[pl.ds(0, HID)], lsem.at[6]),
    ]
    for c in loads:
        c.start()

    def cols_of(c, width):
        return pl.ds(pl.multiple_of(c * width, width), width)

    def wd_copy(c):
        cols = cols_of(c, CW)
        return remote(
            wdf_ref.at[0, :, cols], wd_f.at[pl.ds(HID, HID), cols], ws.at[3 + c], wr.at[3 + c], pair
        )

    weights = [
        remote(winb_ref.at[0], wgu_b.at[1], ws.at[0], wr.at[0], pair),
        remote(wdb_ref.at[0], wd_b.at[pl.ds(HID, HID)], ws.at[1], wr.at[1], pair),
        remote(winf_ref.at[0], wgu_f.at[1], ws.at[2], wr.at[2], pair),
    ] + [wd_copy(c) for c in range(NC)]

    def table(ids_ref, gate_ref, tg):
        ids = ids_ref[...]
        gate = gate_ref[...].astype(F32)
        lane = lax.broadcasted_iota(jnp.int32, (TOK, TOK), 1)
        row = lax.broadcasted_iota(jnp.int32, (TOK, TOK), 0)
        hits = jnp.zeros((TOK, TOK), F32)
        weight = jnp.zeros((TOK, TOK), F32)
        for i, expert in enumerate((mine, 1 - mine)):
            match = ids == expert
            hit = jnp.max(jnp.where(match, 1.0, 0.0), axis=0, keepdims=True)
            w = jnp.sum(jnp.where(match, gate, 0.0), axis=0, keepdims=True)
            here = (row >= CAP * i) & (row < CAP * (i + 1))
            hits = jnp.where(here, hit, hits)
            weight = jnp.where(here, w, weight)
        upper = jnp.where(row <= lane, 1.0, 0.0).astype(BF16)
        order = dot(hits.astype(BF16), upper)
        slot = ((row & (CAP - 1)) + 1).astype(F32)
        tab = jnp.where(order == slot, hits, 0.0)
        tg[...] = (tab * weight).T.astype(BF16)[:, : 2 * CAP]
        return tab.astype(BF16)[: 2 * CAP]

    def normalise(src, gain_ref, keep):
        @pl.loop(0, TOK // 16)
        def _(i):
            rows = pl.ds(pl.multiple_of(i * 16, 16), 16)
            v = src[rows, :].astype(F32)
            r = lax.rsqrt(jnp.sum(v * v, axis=1, keepdims=True) * (1.0 / D) + EPS)
            xh[rows, :] = (v * r * gain_ref[...]).astype(BF16)
            if keep:
                rinv[rows, :] = jnp.broadcast_to(r, (16, TOK))

    def pick(tab, src, a):
        @pl.loop(0, NC)
        def _(c):
            cols = cols_of(c, CW)
            s = dot(tab, src[:, cols]).astype(BF16)
            blk[a, 2 * z, :, cols] = s[:CAP]
            crs[a, :, cols] = s[CAP:]

    def g_copy(a, b, way):
        return remote(
            blk.at[a, b], blk.at[a, b], gs.at[a, way, b], gr.at[a, b], (left, right)[way]
        )

    def x_copy(a):
        return remote(crs.at[a], blk.at[a, 2 * z + 1], xs.at[a], gr.at[a, 2 * z + 1], cross)

    def both_ways(a, b):
        pl.when(has_r)(lambda: g_copy(a, b, 1).start())
        pl.when(has_l)(lambda: g_copy(a, b, 0).start())

    def gather_step(arrays, k):
        for s in range(2):
            for a in arrays:
                @pl.when(z >= k)
                def _():
                    b = 2 * (z - k) + s
                    g_copy(a, b, 1).wait_recv()
                    pl.when(has_r)(lambda: g_copy(a, b, 1).start())

                @pl.when(z + k < NZ)
                def _():
                    b = 2 * (z + k) + s
                    g_copy(a, b, 0).wait_recv()
                    pl.when(has_l)(lambda: g_copy(a, b, 0).start())

    tab = table(idb_ref, gb_ref, tg_b)
    loads[0].wait()
    pick(tab, dy_v, 0)
    loads[1].wait()
    normalise(xb_v, gainb_ref, True)
    pick(tab, xh, 1)
    tab = table(idf_ref, gf_ref, tg_f)
    loads[2].wait()
    normalise(xf_v, gainf_ref, False)
    pick(tab, xh, 2)

    @pl.when(jnp.logical_not(has_prev))
    def _():
        @pl.loop(0, TOK // 16)
        def _(i):
            zero[pl.ds(pl.multiple_of(i * 16, 16), 16), :] = jnp.zeros((16, D), BF16)
        for i, out in enumerate((outf_ref, outb_ref)):
            pltpu.make_async_copy(zero, out, zsem.at[i]).start()

    pl.semaphore_wait(
        bar,
        2 + has_l.astype(jnp.int32) + has_r.astype(jnp.int32)
        + has_prev.astype(jnp.int32) + has_next.astype(jnp.int32),
    )

    second = jnp.logical_not(first)

    def start_weights():
        for c in weights:
            c.start()

    pl.when(first)(start_weights)
    if TURN_AT:
        pl.when(second)(lambda: pl.semaphore_wait(turn, 1))

    def give_turn(at):
        if TURN_AT == at:
            @pl.when(first)
            def _():
                pl.semaphore_signal(turn, inc=1, device_id=behind, device_id_type=MESH)
        if W0_AT == at:
            pl.when(second)(start_weights)

    if W0_AT == 0:
        pl.when(second)(start_weights)
    for a in range(2):
        x_copy(a).start()
        both_ways(a, 2 * z)
    x_copy(2).start()
    for a in range(2):
        x_copy(a).wait_recv()
        both_ways(a, 2 * z + 1)
    gather_step((0, 1), 1)
    give_turn(1)
    gather_step((0, 1), 2)
    give_turn(2)
    both_ways(2, 2 * z)
    x_copy(2).wait_recv()
    both_ways(2, 2 * z + 1)
    gather_step((0, 1), 3)
    give_turn(3)

    def split(g):
        return g // NC, cols_of(lax.rem(g, NC), CW)

    def r_copy(d, way, g):
        a, cols = split(g)
        return remote(
            part.at[a, d, :, cols], got.at[1 - way, a, d, :, cols],
            rs.at[g, d], rr.at[1 - way, g, d], (left, right)[way],
        )

    def add(d, side, g):
        a, cols = split(g)
        part[a, d, :, cols] = (
            part[a, d, :, cols].astype(F32) + got[side, a, d, :, cols].astype(F32)
        ).astype(BF16)

    def edge(g):
        @pl.when(z == 0)
        def _():
            for d in (3, 2, 1):
                r_copy(d, 1, g).start()

        @pl.when(z == NZ - 1)
        def _():
            for d in (0, 1, 2):
                r_copy(d, 0, g).start()

    def pass_on(d, way, g):
        r_copy(d, way, g).wait_recv()
        add(d, 1 - way, g)
        r_copy(d, way, g).start()

    def relay(g):
        @pl.when(z == 1)
        def _():
            pass_on(3, 1, g)
            pass_on(2, 1, g)

        @pl.when(z == 2)
        def _():
            pass_on(0, 0, g)
            pass_on(1, 0, g)

    def relay_again(g):
        pl.when(z == 1)(lambda: pass_on(0, 0, g))
        pl.when(z == 2)(lambda: pass_on(3, 1, g))

    def totals(g):
        a, cols = split(g)
        return remote(
            part.at[a, z, pl.ds(CAP, CAP), cols], tot.at[a, :, cols], ts.at[g], tr.at[g], cross
        )

    def own_sum(g):
        @pl.when(has_l)
        def _():
            r_copy(z, 1, g).wait_recv()
            add(z, 0, g)

        @pl.when(has_r)
        def _():
            r_copy(z, 0, g).wait_recv()
            add(z, 1, g)

        totals(g).start()

    def total_rows(a, cols):
        return jnp.concatenate([part[a, z, pl.ds(0, CAP), cols], tot[a, :, cols]], axis=0)

    def shift_b():
        return remote(o_b, outb_ref, os_b.at[0], or_b.at[0], ahead)

    def shift_f(c):
        cols = cols_of(c, CW)
        return remote(o_f.at[:, cols], outf_ref.at[:, cols], os_f.at[c], or_f.at[c], ahead)

    for i in (3, 4):
        loads[i].wait()
    for i in (0, 1):
        weights[i].wait_recv()
    acc[...] = jnp.zeros_like(acc)
    accd[...] = jnp.zeros_like(accd)

    def gate_up(w, o, rows):
        return jnp.concatenate([w[o, 0, rows, :], w[o, 1, rows, :]], axis=1)

    @pl.loop(0, D // KC)
    def _(c):
        cols = cols_of(c, KC)
        xs_c = blk[1, :, :, cols].reshape(2 * NZ * CAP, KC)
        dy_c = blk[0, :, :, cols].reshape(2 * NZ * CAP, KC)
        for o in range(2):
            acc[o] += dot(xs_c, gate_up(wgu_b, o, cols))
        accd[...] += dot_t(dy_c, wd_b[:, cols])

    for o in range(2):
        a = acc[o, :, :HID]
        b = acc[o, :, HID:]
        dh = accd[:, o * HID : (o + 1) * HID]
        sg = jax.nn.sigmoid(a)
        hid[o, :, :HID] = (dh * b * sg * (1.0 + a * (1.0 - sg))).astype(BF16)
        hid[o, :, HID:] = (dh * a * sg).astype(BF16)

    def part_b(c):
        cols = cols_of(c, CW)
        v = dot_t(hid[0], gate_up(wgu_b, 0, cols)) + dot_t(hid[1], gate_up(wgu_b, 1, cols))
        part[0, :, :, cols] = v.astype(BF16).reshape(NZ, 2 * CAP, CW)

    def hidden_f():
        for i in (5, 6):
            loads[i].wait()
        weights[2].wait_recv()
        acc[...] = jnp.zeros_like(acc)

        @pl.loop(0, D // KC)
        def _(c):
            cols = cols_of(c, KC)
            xs_c = blk[2, :, :, cols].reshape(2 * NZ * CAP, KC)
            for o in range(2):
                acc[o] += dot(xs_c, gate_up(wgu_f, o, cols))

        for o in range(2):
            a = acc[o, :, :HID]
            hid[0, :, o * HID : (o + 1) * HID] = (
                a * jax.nn.sigmoid(a) * acc[o, :, HID:]
            ).astype(BF16)

    def part_f(c):
        wd_copy(c).wait_recv()
        cols = cols_of(c, CW)
        v = dot(hid[0], wd_f[:, cols])
        part[1, :, :, cols] = v.astype(BF16).reshape(NZ, 2 * CAP, CW)

    def finish_b():
        pl.loop(0, NC)(lambda c: totals(c).wait_recv())

        def moe_cols(c, total):
            cols = cols_of(c, CW)
            m = dot(tg_b[...], total_rows(0, cols)) * gainb_ref[:, cols]
            moe[:, cols] = m
            return total + jnp.sum(xb_v[:, cols].astype(F32) * m, axis=1, keepdims=True)

        total = lax.fori_loop(0, NC, moe_cols, jnp.zeros((TOK, 1), F32))
        r = rinv[:, :1]
        scale = r * r * r * (total * (1.0 / D))

        @pl.loop(0, NC)
        def _(c):
            cols = cols_of(c, CW)
            o_b[:, cols] = (
                dy_v[:, cols].astype(F32) + r * moe[:, cols] - xb_v[:, cols].astype(F32) * scale
            ).astype(BF16)

        pl.when(has_next)(lambda: shift_b().start())

    def finish_f(c):
        totals(NC + c).wait_recv()
        cols = cols_of(c, CW)
        o_f[:, cols] = (
            xf_v[:, cols].astype(F32) + dot(tg_f[...], total_rows(1, cols))
        ).astype(BF16)
        pl.when(has_next)(lambda: shift_f(c).start())

    @pl.loop(0, 2 * NC + GAP + 4 * ST)
    def _(i):
        def stage(late, f):
            j = i - late
            back = (j >= 0) & (j < NC)
            front = (j >= NC + GAP) & (j < 2 * NC + GAP)
            pl.when(back | front)(lambda: f(j - GAP * front.astype(jnp.int32)))

        pl.when(i == NC + GAP)(hidden_f)
        pl.when(i < NC)(lambda: part_b(i))
        pl.when((i >= NC + GAP) & (i < 2 * NC + GAP))(lambda: part_f(i - NC - GAP))
        stage(0, edge)
        for k in range(1, NZ):
            pl.when(i == F_AT[k - 1])(lambda: gather_step((2,), k))
        stage(ST, relay)
        stage(2 * ST, relay_again)
        stage(3 * ST, own_sum)
        pl.when(i == NC + 3 * ST + FB)(finish_b)
        pl.when(i >= NC + GAP + 4 * ST)(lambda: finish_f(i - NC - GAP - 4 * ST))

    for c in weights:
        c.wait_send()
    for a in range(3):
        x_copy(a).wait_send()
        for k in range(NZ):
            for s in range(2):
                @pl.when((z >= k) & has_r)
                def _():
                    g_copy(a, 2 * (z - k) + s, 1).wait_send()

                @pl.when((z + k < NZ) & has_l)
                def _():
                    g_copy(a, 2 * (z + k) + s, 0).wait_send()

    @pl.loop(0, 2 * NC)
    def _(g):
        for d in range(NZ):
            pl.when(z < d)(lambda: r_copy(d, 1, g).wait_send())
            pl.when(z > d)(lambda: r_copy(d, 0, g).wait_send())
        totals(g).wait_send()

    @pl.loop(0, NC)
    def _(c):
        pl.when(has_next)(lambda: shift_f(c).wait_send())
        pl.when(has_prev)(lambda: shift_f(c).wait_recv())

    pl.when(has_next)(lambda: shift_b().wait_send())
    pl.when(has_prev)(lambda: shift_b().wait_recv())

    @pl.when(jnp.logical_not(has_prev))
    def _():
        for i, out in enumerate((outf_ref, outb_ref)):
            pltpu.make_async_copy(zero, out, zsem.at[i]).wait()


def local(x, idf, gf, gainf, winf, wdf, xb, dy, idb, gb, gainb, winb, wdb):
    hbm = pl.BlockSpec(memory_space=pl.ANY)
    vmem = pl.BlockSpec(memory_space=pltpu.VMEM)
    dma = pltpu.SemaphoreType.DMA
    blocks = 2 * NZ
    rows = blocks * CAP
    return pl.pallas_call(
        kernel,
        out_shape=[jax.ShapeDtypeStruct((TOK, D), BF16)] * 2,
        in_specs=[
            hbm, vmem, vmem, vmem, hbm, hbm,
            hbm, hbm, vmem, vmem, vmem, hbm, hbm,
        ],
        out_specs=[hbm, hbm],
        scratch_shapes=[
            pltpu.VMEM((TOK, D), BF16),
            pltpu.VMEM((TOK, D), BF16),
            pltpu.VMEM((TOK, D), BF16),
            pltpu.VMEM((TOK, D), BF16),
            pltpu.VMEM((TOK, TOK), F32),
            pltpu.VMEM((TOK, 2 * CAP), BF16),
            pltpu.VMEM((TOK, 2 * CAP), BF16),
            pltpu.VMEM((2, 2, D, HID), BF16),
            pltpu.VMEM((2 * HID, D), BF16),
            pltpu.VMEM((2, 2, D, HID), BF16),
            pltpu.VMEM((2 * HID, D), BF16),
            pltpu.VMEM((3, blocks, CAP, D), BF16),
            pltpu.VMEM((3, CAP, D), BF16),
            pltpu.VMEM((2, NZ, 2 * CAP, D), BF16),
            pltpu.VMEM((2, 2, NZ, 2 * CAP, D), BF16),
            pltpu.VMEM((2, CAP, D), BF16),
            pltpu.VMEM((2, rows, 2 * HID), F32),
            pltpu.VMEM((rows, 2 * HID), F32),
            pltpu.VMEM((2, rows, 2 * HID), BF16),
            pltpu.VMEM((TOK, D), F32),
            pltpu.VMEM((TOK, D), BF16),
            pltpu.VMEM((TOK, D), BF16),
            pltpu.VMEM((TOK, D), BF16),
            dma((7,)),
            dma((3 + NC,)),
            dma((3 + NC,)),
            dma((3, 2, blocks)),
            dma((3, blocks)),
            dma((3,)),
            dma((2 * NC, NZ)),
            dma((2, 2 * NC, NZ)),
            dma((2 * NC,)),
            dma((2 * NC,)),
            dma((1,)),
            dma((1,)),
            dma((NC,)),
            dma((NC,)),
            dma((2,)),
            pltpu.SemaphoreType.REGULAR,
        ],
        compiler_params=pltpu.CompilerParams(
            collective_id=0, has_side_effects=True, vmem_limit_bytes=56 * 2**20
        ),
        cost_estimate=pl.CostEstimate(
            flops=4 * 10**9, bytes_accessed=16 * 10**6, transcendentals=10**5
        ),
    )(x, idf.T, gf.T, gainf, winf, wdf, xb, dy, idb.T, gb.T, gainb, winb, wdb)


def solution(mesh):
    tokens = P(("pipe", "expert"), None)
    w_in = P("pipe", None, None, "expert")
    w_down = P("pipe", "expert", None)
    gain = P("pipe", None)
    return jax.shard_map(
        local,
        mesh=mesh,
        in_specs=(
            tokens, tokens, tokens, gain, w_in, w_down,
            tokens, tokens, tokens, tokens, gain, w_in, w_down,
        ),
        out_specs=(tokens, tokens),
        check_vma=False,
    )
```

time: 237 us -> 186 us (0.78); the launches traced: 232 us -> 184 us
  Pallas kernels: 223 us -> 181 us
  local copies, waits for them, and re-layouts: 8.76 us -> 3.17 us
    pallas_call x1, Pallas kernels: 223 us -> 181 us  [local(): pl.pallas_call(kernel, out_shape=[jax.ShapeDtypeStruct((TOK, D), BF16)] *...]
    unnamed x8 -> x4, local copies, waits for them, and re-layouts: 8.76 us -> 3.17 us
where the time goes in v2:
time: 186 us; the launch traced here: 184 us
  Pallas kernels  181 us (97%)
  local copies, waits for them, and re-layouts  3.17 us (2%)
    pallas_call x1, Pallas kernels, local(): pl.pallas_call(kernel, out_shape=[jax.ShapeDtypeStruct((TOK, D), BF16)] *...  181 us

profile of v2, /device:TPU:16, one launch (start us, length us, event | category | flops | bytes accessed | tf_op | source)
XLA Modules:
  0.0 184.4 jit_solution(4157229635210989913)
XLA Ops:
  0.6 180.6 %shard_map.140 = (bf16[128,3584]{1,0:T(8,128)(2,1)}, bf16[128,3584]{1,0:T(8,128)(2,1)}) custom-call(bf16[128,3584]{1,0:T(8,128)(2,1)} %x_ref.1, s32[8,128]{1,0:T(8,128)} %bitcast.4, bf16[8,128]{1,0:T(8,128)(2,1)} %bitcast.6, f32[1,3584]{1,0:T(1,128)} %gainf_ref.1, bf16[1,2,3584,128]{3,2,1,0:T(8,128)(2,1)} %winf_ref.1, bf16[1,128,3584]{2,1,0:T(8,128)(2,1)} %wdf_ref.1, ...), custom_call_target="tpu_custom_call" | custom-call | flops 4000000000 | bytes 16000000 | tf_op jit(solution)/shard_map/pallas_call | solution.py:462
  181.3 0.0 copy-start
  181.3 2.2 %copy.17 = bf16[128,3584]{1,0:T(8,128)(2,1)} copy(bf16[128,3584]{1,0:T(8,128)(2,1)} %get-tuple-element.4) | data formatting | bytes 1835008
  183.5 0.0 copy-done
  183.5 0.9 copy.18
Async XLA Ops:
  181.3 2.3 %copy-start = (bf16[128,3584]{1,0:T(8,128)(2,1)S(1)}, bf16[128,3584]{1,0:T(8,128)(2,1)}, u32[]{:S(2)}) copy-start(bf16[128,3584]{1,0:T(8,128)(2,1)} %get-tuple-element.5) | copy-start | bytes 2752516

commit v3 on v2

--- a/solution.py
+++ b/solution.py
@@ -346,17 +346,18 @@
     def hidden_f():
         for i in (5, 6):
             loads[i].wait()
-        weights[2].wait_recv()
         acc[...] = jnp.zeros_like(acc)
 
-        @pl.loop(0, D // KC)
-        def _(c):
-            cols = cols_of(c, KC)
-            xs_c = blk[2, :, :, cols].reshape(2 * NZ * CAP, KC)
-            for o in range(2):
+        for o in range(2):
+            if o == 1:
+                weights[2].wait_recv()
+
+            @pl.loop(0, D // KC)
+            def _(c):
+                cols = cols_of(c, KC)
+                xs_c = blk[2, :, :, cols].reshape(2 * NZ * CAP, KC)
                 acc[o] += dot(xs_c, gate_up(wgu_f, o, cols))
 
-        for o in range(2):
             a = acc[o, :, :HID]
             hid[0, :, o * HID : (o + 1) * HID] = (
                 a * jax.nn.sigmoid(a) * acc[o, :, HID:]

time: 186 us -> 187 us (level)
  no operation moved by 1% of the time
where the time goes in v3:
time: 187 us; the launch traced here: 185 us
  Pallas kernels  181 us (97%)
  local copies, waits for them, and re-layouts  3.17 us (2%)
    pallas_call x1, Pallas kernels, local(): pl.pallas_call(kernel, out_shape=[jax.ShapeDtypeStruct((TOK, D), BF16)] *...  181 us

profile of v3, /device:TPU:16, one launch (start us, length us, event | category | flops | bytes accessed | tf_op | source)
XLA Modules:
  0.0 185.1 jit_solution(8295289176846197154)
XLA Ops:
  0.6 181.3 %shard_map.140 = (bf16[128,3584]{1,0:T(8,128)(2,1)}, bf16[128,3584]{1,0:T(8,128)(2,1)}) custom-call(bf16[128,3584]{1,0:T(8,128)(2,1)} %x_ref.1, s32[8,128]{1,0:T(8,128)} %bitcast.4, bf16[8,128]{1,0:T(8,128)(2,1)} %bitcast.6, f32[1,3584]{1,0:T(1,128)} %gainf_ref.1, bf16[1,2,3584,128]{3,2,1,0:T(8,128)(2,1)} %winf_ref.1, bf16[1,128,3584]{2,1,0:T(8,128)(2,1)} %wdf_ref.1, ...), custom_call_target="tpu_custom_call" | custom-call | flops 4000000000 | bytes 16000000 | tf_op jit(solution)/shard_map/pallas_call | solution.py:463
  182.0 0.0 copy-start
  182.0 2.2 %copy.17 = bf16[128,3584]{1,0:T(8,128)(2,1)} copy(bf16[128,3584]{1,0:T(8,128)(2,1)} %get-tuple-element.4) | data formatting | bytes 1835008
  184.2 0.0 copy-done
  184.2 0.9 copy.18
Async XLA Ops:
  182.0 2.3 %copy-start = (bf16[128,3584]{1,0:T(8,128)(2,1)S(1)}, bf16[128,3584]{1,0:T(8,128)(2,1)}, u32[]{:S(2)}) copy-start(bf16[128,3584]{1,0:T(8,128)(2,1)} %get-tuple-element.5) | copy-start | bytes 2752516
